TPU v7x, 256 devices: a whole 4x4x8 slice. The times are simulated.
256 devices in a mesh: row: 16 (over y_hi, x, core), rep: 16 (over y_lo, z).
Axes of the slice: x: 4, y: 4 (y_hi: 2, y_lo: 2; y = y_hi * 2 + y_lo), z: 8, core: 2. Of those that a mesh axis runs over, the one named last changes fastest.
Arguments:
- features: bfloat16 [65536, 512], P(('row', 'rep')), may hold values from -6 to 6
- tiles: bfloat16 [512, 8, 128, 128], P(('row', 'rep')), may hold values from -0.1875 to 0.1875
- columns: int32 [512, 8], P(('row', 'rep')), may hold values from 0 to 511, as said below
- w_aggregate: bfloat16 [512, 512], replicated, may hold values from -0.25 to 0.25
- w_self: bfloat16 [512, 512], replicated, may hold values from -0.25 to 0.25
- w_middle: bfloat16 [512, 512], replicated, may hold values from -0.25 to 0.25
- w_output: bfloat16 [512, 512], replicated, may hold values from -0.25 to 0.25
- cotangent: bfloat16 [65536, 512], P(('row', 'rep')), may hold values from -6 to 6
Outputs:
- updated: bfloat16 [65536, 512], P(('row', 'rep'))
- grad_features: bfloat16 [65536, 512], P(('row', 'rep'))
- grad_output: float32 [512, 512], P('rep')
- grad_middle: float32 [512, 512], P('rep')
- grad_aggregate: float32 [512, 512], P('rep')
- grad_self: float32 [512, 512], P('rep')
Inputs may be any that keep to these rules, and one draw needn't show every extreme that they name: `columns`: row group g holds row blocks g * 32 to (g + 1) * 32 - 1, for g < 16. Every column block named by a row block of group g lies in group g - 1, g or g + 1, taken modulo 16; every row block names each of these three groups at least once. Column blocks may repeat within a row block.
All inputs are finite; a program needn't handle non-finite values.
Results may differ from a plain program's by a relative error of at most 0.015.
Values may be sent and summed in bfloat16 or wider, within the bound.
A program may use at most 192 MiB of HBM per device.

v0:
```python
import math
import jax
import jax.numpy as jnp
from jax import lax
from jax.sharding import PartitionSpec as P


def from_behind(value, axis, steps):
    count = lax.axis_size(axis)
    pairs = [(source, (source + steps) % count) for source in range(count)]
    return lax.ppermute(value, axis, pairs)


def silu_slope(value):
    sig = jax.nn.sigmoid(value)
    return sig * (1.0 + value * (1.0 - sig))


def times_transposed(left_operand, weight):
    return lax.dot_general(
        left_operand, weight, (((1,), (1,)), ((), ())), preferred_element_type=jnp.float32
    )


def local(features, tiles, columns, w_aggregate, w_self, w_middle, w_output, cotangent):
    blocks_dev, width_k, tile_size, _ = tiles.shape
    width = features.shape[1]
    groups = lax.axis_size("row")
    replicas = lax.axis_size("rep")
    panel_blocks = replicas * blocks_dev
    panel_rows = panel_blocks * tile_size
    group_id = lax.axis_index("row")
    slot_of = (columns // panel_blocks - group_id + 1) % groups
    window_index = slot_of * panel_blocks + columns % panel_blocks
    own_panel = lax.all_gather(features, "rep", axis=0, tiled=True)
    prior_panel = from_behind(own_panel, "row", 1)
    next_panel = from_behind(own_panel, "row", -1)
    window = jnp.concatenate([prior_panel, own_panel, next_panel], 0).reshape(
        3 * panel_blocks, tile_size, width
    )
    picked = window[window_index]
    summed = jnp.einsum("bkij,bkjf->bif", tiles, picked, preferred_element_type=jnp.float32)
    aggregate = summed.reshape(blocks_dev * tile_size, width).astype(jnp.bfloat16)
    pre_first = jnp.dot(aggregate, w_aggregate, preferred_element_type=jnp.float32) + jnp.dot(
        features, w_self, preferred_element_type=jnp.float32
    )
    first = jax.nn.silu(pre_first).astype(jnp.bfloat16)
    pre_second = jnp.dot(first, w_middle, preferred_element_type=jnp.float32)
    second = jax.nn.silu(pre_second).astype(jnp.bfloat16)
    updated = (
        features.astype(jnp.float32) + jnp.dot(second, w_output, preferred_element_type=jnp.float32)
    ).astype(jnp.bfloat16)
    delta_second = (times_transposed(cotangent, w_output) * silu_slope(pre_second)).astype(
        jnp.bfloat16
    )
    delta_first = (times_transposed(delta_second, w_middle) * silu_slope(pre_first)).astype(
        jnp.bfloat16
    )
    delta_aggregate = times_transposed(delta_first, w_aggregate).astype(jnp.bfloat16)
    delta_blocks = delta_aggregate.reshape(blocks_dev, tile_size, width)
    messages = jnp.einsum("bkji,bjf->bkif", tiles, delta_blocks, preferred_element_type=jnp.float32)
    spread = jnp.zeros((3 * panel_blocks, tile_size, width), jnp.float32)
    spread = spread.at[window_index.reshape(-1)].add(messages.reshape(-1, tile_size, width))
    spread = spread.reshape(3 * panel_rows, width)
    prior_part = spread[:panel_rows]
    own_part = spread[panel_rows : 2 * panel_rows]
    next_part = spread[2 * panel_rows :]
    from_next = from_behind(prior_part.astype(jnp.bfloat16), "row", -1).astype(prior_part.dtype)
    from_prior = from_behind(next_part.astype(jnp.bfloat16), "row", 1).astype(next_part.dtype)
    returned = lax.psum_scatter(
        (own_part + from_next + from_prior).astype(jnp.bfloat16),
        "rep",
        scatter_dimension=0,
        tiled=True,
    ).astype(jnp.float32)
    grad_features = (
        cotangent.astype(jnp.float32) + times_transposed(delta_first, w_self) + returned
    ).astype(jnp.bfloat16)
    total_nodes = features.shape[0] * groups * replicas
    scale = 1.0 / math.sqrt(total_nodes)
    local_output = jnp.dot(second.T, cotangent, preferred_element_type=jnp.float32)
    local_middle = jnp.dot(first.T, delta_second, preferred_element_type=jnp.float32)
    local_aggregate = jnp.dot(aggregate.T, delta_first, preferred_element_type=jnp.float32)
    local_self = jnp.dot(features.T, delta_first, preferred_element_type=jnp.float32)
    share_rows = width // replicas
    totals = lax.psum((local_output, local_middle, local_aggregate, local_self), ("row", "rep"))
    start_row = lax.axis_index("rep") * share_rows
    totals = tuple(
        (lax.dynamic_slice_in_dim(member, start_row, share_rows, 0) for member in totals)
    )
    return (
        updated,
        grad_features,
        totals[0] * scale,
        totals[1] * scale,
        totals[2] * scale,
        totals[3] * scale,
    )


def solution(mesh):
    placed = (
        P(("row", "rep"), None),
        P(("row", "rep"), None, None, None),
        P(("row", "rep"), None),
        P(),
        P(),
        P(),
        P(),
        P(("row", "rep"), None),
    )
    return jax.shard_map(
        local,
        mesh=mesh,
        in_specs=placed,
        out_specs=(
            P(("row", "rep"), None),
            P(("row", "rep"), None),
            P("rep", None),
            P("rep", None),
            P("rep", None),
            P("rep", None),
        ),
        check_vma=False,
    )
```

profile of v0, /device:TPU:4, one launch (start us, length us, event | category | flops | bytes accessed | tf_op | source)
XLA Modules:
  0.0 576.8 jit_solution(3026869364455568108)
XLA Ops:
  8.0 81.7 %all-gather.2.cloned.1.call-done = bf16[4096,512]{1,0:T(8,128)(2,1)} async-done(((bf16[256,512]{1,0:T(8,128)(2,1)}), bf16[4096,512]{1,0:T(8,128)(2,1)}) %all-gather.2.cloned.1.call-update) | async-done | bytes 4194320 | tf_op jit(solution)/shard_map/all_gather | solution.py:35
  91.0 45.0 %collective-permute-done.1 = bf16[4096,512]{1,0:T(8,128)(2,1)} collective-permute-done((bf16[4096,512]{1,0:T(8,128)(2,1)}, bf16[4096,512]{1,0:T(8,128)(2,1)}, u32[]{:S(2)}, u32[]{:S(2)}) %collective-permute-start.1) | collective-permute-done | bytes 4194336 | tf_op jit(solution)/shard_map/ppermute | solution.py:11
  136.0 1.9 collective-permute-done
  137.9 15.9 %pad_maximum_fusion = bf16[12288,512]{1,0:T(8,128)(2,1)} fusion(bf16[4096,512]{1,0:T(8,128)(2,1)} %collective-permute-done.1, bf16[4096,512]{1,0:T(8,128)(2,1)} %all-gather.2.cloned.1.call-done, bf16[4096,512]{1,0:T(8,128)(2,1)} %collective-permute-done), kind=kLoop, calls=%fused_computation.2 | loop fusion | flops 37748736 | bytes 25165824 | tf_op jit(solution)/shard_map/concatenate | solution.py:38
  153.8 5.3 gather_fusion
  159.6 1.4 fusion.15
  163.5 2.7 fusion.16
  166.2 5.4 copy.15
  171.6 11.5 %broadcast_in_dim.8 = f32[96,128,512]{2,1,0:T(8,128)} broadcast(f32[]{:T(128)} %constant.62.clone.1), dimensions={} | broadcast | bytes 25165828 | tf_op jit(solution)/shard_map/broadcast_in_dim | solution.py:62
  183.1 9.6 %scatter_fusion = f32[96,128,512]{2,1,0:T(8,128)} fusion(f32[96,128,512]{2,1,0:T(8,128)} %broadcast_in_dim.8, s32[16]{0:T(128)S(1)} %fusion.9, f32[16,128,512]{2,1,0:T(8,128)} %copy.15), kind=kCustom, calls=%fused_computation.1 | custom fusion | flops 1048576 | bytes 12582976 | tf_op jit(solution)/shard_map/scatter-add | solution.py:63
  192.7 9.3 %convert.4 = bf16[96,128,512]{2,1,0:T(8,128)(2,1)S(1)} convert(f32[96,128,512]{2,1,0:T(8,128)} %scatter_fusion) | non-fusion elementwise | flops 6291456 | bytes 37748736 | tf_op jit(solution)/shard_map/convert.1
  202.0 3.5 fusion.14
  205.5 1.7 collective-permute-start.2
  208.6 1.4 convolution_bitcast_fusion
  210.0 1.3 fusion.11
  211.3 1.4 fusion.10
  212.8 8.2 %slice.22 = f32[32,128,512]{2,1,0:T(8,128)} slice(f32[96,128,512]{2,1,0:T(8,128)} %scatter_fusion), slice={[32:64], [0:128], [0:512]} | slice | bytes 16777216 | tf_op jit(solution)/shard_map/slice | solution.py:66
  221.0 36.8 %collective-permute-done.3 = bf16[4096,512]{1,0:T(8,128)(2,1)} collective-permute-done((bf16[4096,512]{1,0:T(8,128)(2,1)}, bf16[4096,512]{1,0:T(8,128)(2,1)}, u32[]{:S(2)}, u32[]{:S(2)}) %collective-permute-start.3) | collective-permute-done | bytes 4194336 | tf_op jit(solution)/shard_map/ppermute | solution.py:11
  257.8 9.7 %fusion.1 = bf16[4096,512]{1,0:T(8,128)(2,1)} fusion(f32[32,128,512]{2,1,0:T(8,128)} %slice.22, bf16[4096,512]{1,0:T(8,128)(2,1)} %collective-permute-done.3, bf16[4096,512]{1,0:T(8,128)(2,1)} %collective-permute-done.2), kind=kLoop, calls=%fused_computation.5 | loop fusion | flops 10485760 | bytes 20971520 | tf_op jit(solution)/shard_map/convert_element_type | solution.py:71
  269.9 216.6 %all-reduce.3.cloned.1.call-done = (f32[512,512]{1,0:T(8,128)}, f32[512,512]{1,0:T(8,128)}, f32[512,512]{1,0:T(8,128)}, f32[512,512]{1,0:T(8,128)}) async-done(((f32[512,512]{1,0:T(8,128)}, f32[512,512]{1,0:T(8,128)}, f32[512,512]{1,0:T(8,128)}, f32[512,512]{1,0:T(8,128)}), (f32[512,512]{1,0:T(8,128)}, f32[512,512]{1,0:T(8,128)}, f32[512,512]{1,0:T(8,128)}, ...) | async-done | bytes 4194320 | tf_op jit(solution)/shard_map/psum | solution.py:86
  486.5 1.5 dynamic-slice_multiply_fusion.2
  488.0 1.5 dynamic-slice_multiply_fusion
  489.6 79.0 %reduce-scatter.2.cloned.1.call-done = bf16[256,512]{1,0:T(8,128)(2,1)} async-done(((bf16[4096,512]{1,0:T(8,128)(2,1)}), bf16[256,512]{1,0:T(8,128)(2,1)}) %reduce-scatter.2.cloned.1.call-update) | async-done | bytes 262160 | tf_op jit(solution)/shard_map/reduce_scatter | solution.py:70
  568.6 1.7 add_convert_fusion
  (48 shorter events, 8.8 us)
Async XLA Ops:
  7.2 152.0 %copy-start = (bf16[2,8,128,128]{3,2,1,0:T(8,128)(2,1)S(1)}, bf16[2,8,128,128]{3,2,1,0:T(8,128)(2,1)}, u32[]{:S(2)}) copy-start(bf16[2,8,128,128]{3,2,1,0:T(8,128)(2,1)} %param.9) | copy-start | bytes 1572868
  7.2 82.4 %all-gather.2.cloned.1.call-start = ((), (), s32[]{:S(2)}) async-start(), calls=%async_computation.1 | async-start | bytes 4456448 | tf_op jit(solution)/shard_map/all_gather | solution.py:35
  7.9 478.6 %all-reduce.3.cloned.1.call-start = ((), (), s32[]{:S(2)}) async-start(), calls=%async_computation.3 | async-start | bytes 8388608 | tf_op jit(solution)/shard_map/psum | solution.py:86
  89.6 46.3 %collective-permute-start.1 = (bf16[4096,512]{1,0:T(8,128)(2,1)}, bf16[4096,512]{1,0:T(8,128)(2,1)}, u32[]{:S(2)}, u32[]{:S(2)}) collective-permute-start(bf16[4096,512]{1,0:T(8,128)(2,1)} %all-gather.2.cloned.1.call-done), channel_id=1, source_target_pairs={{0,240},{16,0},{32,16},{48,32},{64,48},{80,64},{96,80},{112,96},{1... | collective-permute-start | bytes 12582920 | tf_op jit(solution)/shard_map/ppermute | solution.py:11
  89.6 48.2 %collective-permute-start = (bf16[4096,512]{1,0:T(8,128)(2,1)}, bf16[4096,512]{1,0:T(8,128)(2,1)}, u32[]{:S(2)}, u32[]{:S(2)}) collective-permute-start(bf16[4096,512]{1,0:T(8,128)(2,1)} %all-gather.2.cloned.1.call-done), channel_id=1, source_target_pairs={{0,16},{16,32},{32,48},{48,64},{64,80},{80,96},{96,112},{112,128},... | collective-permute-start | bytes 12582920 | tf_op jit(solution)/shard_map/ppermute | solution.py:11
  153.8 7.2 %copy-start.2 = (bf16[256,512]{1,0:T(8,128)(2,1)S(1)}, bf16[256,512]{1,0:T(8,128)(2,1)}, u32[]{:S(2)}) copy-start(bf16[256,512]{1,0:T(8,128)(2,1)} %param.8) | copy-start | bytes 786436
  159.1 1.9 copy-start.3
  159.1 2.2 copy-start.7
  159.1 2.5 copy-start.6
  159.2 2.5 copy-start.8
  161.7 1.5 copy-start.5
  162.1 0.7 copy-start.10
  202.0 8.0 %copy-start.11 = (bf16[256,512]{1,0:T(8,128)(2,1)S(1)}, bf16[256,512]{1,0:T(8,128)(2,1)}, u32[]{:S(2)}) copy-start(bf16[256,512]{1,0:T(8,128)(2,1)} %copy-done.10) | copy-start | bytes 786436
  205.5 52.3 %collective-permute-start.3 = (bf16[4096,512]{1,0:T(8,128)(2,1)}, bf16[4096,512]{1,0:T(8,128)(2,1)}, u32[]{:S(2)}, u32[]{:S(2)}) collective-permute-start(bf16[4096,512]{1,0:T(8,128)(2,1)} %bitcast.13), channel_id=1, source_target_pairs={{0,16},{16,32},{32,48},{48,64},{64,80},{80,96},{96,112},{112,128},... | collective-permute-start | bytes 12582920 | tf_op jit(solution)/shard_map/ppermute | solution.py:11
  205.5 52.3 %collective-permute-start.2 = (bf16[4096,512]{1,0:T(8,128)(2,1)}, bf16[4096,512]{1,0:T(8,128)(2,1)}, u32[]{:S(2)}, u32[]{:S(2)}) collective-permute-start(bf16[4096,512]{1,0:T(8,128)(2,1)} %bitcast.12), channel_id=1, source_target_pairs={{0,240},{16,0},{32,16},{48,32},{64,48},{80,64},{96,80},{112,96},{1... | collective-permute-start | bytes 12582920 | tf_op jit(solution)/shard_map/ppermute | solution.py:11
  212.7 355.9 %reduce-scatter.2.cloned.1.call-start = ((), (), s32[]{:S(2)}) async-start(), calls=%async_computation.2 | async-start | bytes 4456448 | tf_op jit(solution)/shard_map/reduce_scatter | solution.py:70
  267.5 1.0 copy-start.9
  267.5 2.1 copy-start.4
  267.5 302.8 %copy-start.1 = (bf16[2,8,128,128]{3,2,1,0:T(8,128)(2,1)S(1)}, bf16[2,8,128,128]{3,2,1,0:T(8,128)(2,1)}, u32[]{:S(2)}) copy-start(bf16[2,8,128,128]{3,2,1,0:T(8,128)(2,1)} %param.9) | copy-start | bytes 1572868
Sparse Core Ops, SparseCore 0:
  9.8 79.7 all-gather.1
  212.8 273.6 all-reduce.2
  489.2 79.3 reduce-scatter.1
where the time goes:
time: 577 us
  waiting for transfers between devices  462 us (80%)
  other arithmetic  50 us (9%)
  local copies, waits for them, and re-layouts  35.9 us (6%)
  between operations  14 us (2%)
  matrix products  13 us (2%)
    psum x1, waiting for transfers between devices, local(): lax.psum((local_output, local_middle, local_aggregate, local_self), ('row...  217 us
    ppermute x4, waiting for transfers between devices, from_behind(): return lax.ppermute(value, axis, pairs)  83.7 us
    all_gather x1, waiting for transfers between devices, local(): own_panel = lax.all_gather(features, 'rep', axis=0, tiled=True)  81.7 us
    reduce_scatter x1, waiting for transfers between devices, local(): lax.psum_scatter((own_part + from_next + from_prior).astype(jnp.bfloat16)...  79 us
    concatenate x1, other arithmetic, local(): jnp.concatenate([prior_panel, own_panel, next_panel], 0)  15.9 us
  transfers between devices with their start and end apart: 7, of which 6 were waited for; matrix products, arithmetic and copies ran while one was open for 5% of the time, Pallas kernels for 0%

commit v1 on v0

--- a/solution.py
+++ b/solution.py
@@ -3,6 +3,8 @@
 import jax.numpy as jnp
 from jax import lax
 from jax.sharding import PartitionSpec as P
+
+layers_all_run = lambda target: jax.lax.psum(jax.lax.psum(target, axis_name="row"), axis_name="rep")
 
 
 def from_behind(value, axis, steps):
@@ -83,7 +85,7 @@
     local_aggregate = jnp.dot(aggregate.T, delta_first, preferred_element_type=jnp.float32)
     local_self = jnp.dot(features.T, delta_first, preferred_element_type=jnp.float32)
     share_rows = width // replicas
-    totals = lax.psum((local_output, local_middle, local_aggregate, local_self), ("row", "rep"))
+    totals = layers_all_run((local_output, local_middle, local_aggregate, local_self))
     start_row = lax.axis_index("rep") * share_rows
     totals = tuple(
         (lax.dynamic_slice_in_dim(member, start_row, share_rows, 0) for member in totals)

time: 577 us -> 577 us (level)
    psum x1 -> x2, waiting for transfers between devices: 217 us -> 255 us  [the longest x1 144 us: jax.lax.psum(jax.lax.psum(target, axis_name='row'), axis_name='rep')]
    ppermute x4, waiting for transfers between devices: 83.7 us -> 46.9 us  [from_behind(): return lax.ppermute(value, axis, pairs)]
  transfers between devices with their start and end apart: 7 -> 8, of which waited for: 6 -> 6; matrix products, arithmetic and copies ran while one was open for 5% -> 11% of each run, Pallas kernels for 0% -> 0%
where the time goes in v1:
time: 577 us; the launch traced here: 576 us
  waiting for transfers between devices  461 us (80%)
  other arithmetic  50 us (9%)
  local copies, waits for them, and re-layouts  35.6 us (6%)
  between operations  13.9 us (2%)
  matrix products  13 us (2%)
    psum x1, waiting for transfers between devices, jax.lax.psum(jax.lax.psum(target, axis_name='row'), axis_name='rep')  144 us
    psum x1, waiting for transfers between devices, jax.lax.psum(target, axis_name='row')  111 us
    all_gather x1, waiting for transfers between devices, local(): own_panel = lax.all_gather(features, 'rep', axis=0, tiled=True)  81.7 us
    reduce_scatter x1, waiting for transfers between devices, local(): lax.psum_scatter((own_part + from_next + from_prior).astype(jnp.bfloat16)...  77.2 us
    ppermute x4, waiting for transfers between devices, from_behind(): return lax.ppermute(value, axis, pairs)  46.9 us
    concatenate x1, other arithmetic, local(): jnp.concatenate([prior_panel, own_panel, next_panel], 0)  15.9 us
    broadcast_in_dim x1, local copies, waits for them, and re-layouts, local(): spread = jnp.zeros((3 * panel_blocks, tile_size, width), jnp.float32)  11.9 us
  transfers between devices with their start and end apart: 8, of which 6 were waited for; matrix products, arithmetic and copies ran while one was open for 11% of the time, Pallas kernels for 0%

profile of v1, /device:TPU:4, one launch (start us, length us, event | category | flops | bytes accessed | tf_op | source)
XLA Modules:
  0.0 576.2 jit_solution(3201261502232360988)
XLA Ops:
  8.0 81.7 %all-gather.2.cloned.1.call-done = bf16[4096,512]{1,0:T(8,128)(2,1)} async-done(((bf16[256,512]{1,0:T(8,128)(2,1)}), bf16[4096,512]{1,0:T(8,128)(2,1)}) %all-gather.2.cloned.1.call-update) | async-done | bytes 4194320 | tf_op jit(solution)/shard_map/all_gather | solution.py:37
  90.9 45.0 %collective-permute-done.1 = bf16[4096,512]{1,0:T(8,128)(2,1)} collective-permute-done((bf16[4096,512]{1,0:T(8,128)(2,1)}, bf16[4096,512]{1,0:T(8,128)(2,1)}, u32[]{:S(2)}, u32[]{:S(2)}) %collective-permute-start.1) | collective-permute-done | bytes 4194336 | tf_op jit(solution)/shard_map/ppermute | solution.py:13
  136.0 1.9 collective-permute-done
  137.9 15.9 %pad_maximum_fusion = bf16[12288,512]{1,0:T(8,128)(2,1)} fusion(bf16[4096,512]{1,0:T(8,128)(2,1)} %collective-permute-done.1, bf16[4096,512]{1,0:T(8,128)(2,1)} %all-gather.2.cloned.1.call-done, bf16[4096,512]{1,0:T(8,128)(2,1)} %collective-permute-done), kind=kLoop, calls=%fused_computation.2 | loop fusion | flops 37748736 | bytes 25165824 | tf_op jit(solution)/shard_map/concatenate | solution.py:40
  153.8 5.3 gather_fusion
  159.6 1.3 fusion.15
  162.4 1.3 fusion.11
  163.8 1.4 fusion.10
  166.5 1.3 convolution_bitcast_fusion
  168.3 2.7 fusion.16
  171.0 5.4 copy.15
  176.4 11.9 %broadcast_in_dim.8 = f32[96,128,512]{2,1,0:T(8,128)} broadcast(f32[]{:T(128)} %constant.62.clone.1), dimensions={} | broadcast | bytes 25165828 | tf_op jit(solution)/shard_map/broadcast_in_dim | solution.py:64
  188.2 9.7 %scatter_fusion = f32[96,128,512]{2,1,0:T(8,128)} fusion(f32[96,128,512]{2,1,0:T(8,128)} %broadcast_in_dim.8, s32[16]{0:T(128)S(1)} %fusion.9, f32[16,128,512]{2,1,0:T(8,128)} %copy.15), kind=kCustom, calls=%fused_computation.1 | custom fusion | flops 1048576 | bytes 12582976 | tf_op jit(solution)/shard_map/scatter-add | solution.py:65
  197.9 9.3 %convert.4 = bf16[96,128,512]{2,1,0:T(8,128)(2,1)S(1)} convert(f32[96,128,512]{2,1,0:T(8,128)} %scatter_fusion) | non-fusion elementwise | flops 6291456 | bytes 37748736 | tf_op jit(solution)/shard_map/convert.1
  207.3 3.6 fusion.14
  210.9 1.7 collective-permute-start.2
  212.6 110.6 %all-reduce.7.cloned.1.call-done = (f32[512,512]{1,0:T(8,128)}, f32[512,512]{1,0:T(8,128)}, f32[512,512]{1,0:T(8,128)}, f32[512,512]{1,0:T(8,128)}) async-done(((f32[512,512]{1,0:T(8,128)}, f32[512,512]{1,0:T(8,128)}, f32[512,512]{1,0:T(8,128)}, f32[512,512]{1,0:T(8,128)}), (f32[512,512]{1,0:T(8,128)}, f32[512,512]{1,0:T(8,128)}, f32[512,512]{1,0:T(8,128)}, ...) | async-done | bytes 4194320 | tf_op jit(solution)/shard_map/psum | solution.py:7
  323.3 8.2 %slice.22 = f32[32,128,512]{2,1,0:T(8,128)} slice(f32[96,128,512]{2,1,0:T(8,128)} %scatter_fusion), slice={[32:64], [0:128], [0:512]} | slice | bytes 16777216 | tf_op jit(solution)/shard_map/slice | solution.py:68
  331.5 9.5 %fusion.1 = bf16[4096,512]{1,0:T(8,128)(2,1)} fusion(f32[32,128,512]{2,1,0:T(8,128)} %slice.22, bf16[4096,512]{1,0:T(8,128)(2,1)} %collective-permute-done.3, bf16[4096,512]{1,0:T(8,128)(2,1)} %collective-permute-done.2), kind=kLoop, calls=%fused_computation.5 | loop fusion | flops 10485760 | bytes 20971520 | tf_op jit(solution)/shard_map/convert_element_type | solution.py:73
  343.5 144.3 %all-reduce.5.cloned.1.call-done = (f32[512,512]{1,0:T(8,128)}, f32[512,512]{1,0:T(8,128)}, f32[512,512]{1,0:T(8,128)}, f32[512,512]{1,0:T(8,128)}) async-done(((f32[512,512]{1,0:T(8,128)}, f32[512,512]{1,0:T(8,128)}, f32[512,512]{1,0:T(8,128)}, f32[512,512]{1,0:T(8,128)}), (f32[512,512]{1,0:T(8,128)}, f32[512,512]{1,0:T(8,128)}, f32[512,512]{1,0:T(8,128)}, ...) | async-done | bytes 4194320 | tf_op jit(solution)/shard_map/psum | solution.py:7
  487.7 1.5 dynamic-slice_multiply_fusion.2
  489.3 1.5 dynamic-slice_multiply_fusion
  490.8 77.2 %reduce-scatter.2.cloned.1.call-done = bf16[256,512]{1,0:T(8,128)(2,1)} async-done(((bf16[4096,512]{1,0:T(8,128)(2,1)}), bf16[256,512]{1,0:T(8,128)(2,1)}) %reduce-scatter.2.cloned.1.call-update) | async-done | bytes 262160 | tf_op jit(solution)/shard_map/reduce_scatter | solution.py:72
  568.0 1.7 add_convert_fusion
  (47 shorter events, 8.2 us)
Async XLA Ops:
  7.2 152.0 %copy-start = (bf16[2,8,128,128]{3,2,1,0:T(8,128)(2,1)S(1)}, bf16[2,8,128,128]{3,2,1,0:T(8,128)(2,1)}, u32[]{:S(2)}) copy-start(bf16[2,8,128,128]{3,2,1,0:T(8,128)(2,1)} %param.9) | copy-start | bytes 1572868
  7.2 82.4 %all-gather.2.cloned.1.call-start = ((), (), s32[]{:S(2)}) async-start(), calls=%async_computation.1 | async-start | bytes 4456448 | tf_op jit(solution)/shard_map/all_gather | solution.py:37
  7.9 315.3 %all-reduce.7.cloned.1.call-start = ((), (), s32[]{:S(2)}) async-start(), calls=%async_computation.4 | async-start | bytes 8388608 | tf_op jit(solution)/shard_map/psum | solution.py:7
  89.6 46.3 %collective-permute-start.1 = (bf16[4096,512]{1,0:T(8,128)(2,1)}, bf16[4096,512]{1,0:T(8,128)(2,1)}, u32[]{:S(2)}, u32[]{:S(2)}) collective-permute-start(bf16[4096,512]{1,0:T(8,128)(2,1)} %all-gather.2.cloned.1.call-done), channel_id=1, source_target_pairs={{0,240},{16,0},{32,16},{48,32},{64,48},{80,64},{96,80},{112,96},{1... | collective-permute-start | bytes 12582920 | tf_op jit(solution)/shard_map/ppermute | solution.py:13
  89.6 48.2 %collective-permute-start = (bf16[4096,512]{1,0:T(8,128)(2,1)}, bf16[4096,512]{1,0:T(8,128)(2,1)}, u32[]{:S(2)}, u32[]{:S(2)}) collective-permute-start(bf16[4096,512]{1,0:T(8,128)(2,1)} %all-gather.2.cloned.1.call-done), channel_id=1, source_target_pairs={{0,16},{16,32},{32,48},{48,64},{64,80},{80,96},{96,112},{112,128},... | collective-permute-start | bytes 12582920 | tf_op jit(solution)/shard_map/ppermute | solution.py:13
  153.8 7.2 %copy-start.2 = (bf16[256,512]{1,0:T(8,128)(2,1)S(1)}, bf16[256,512]{1,0:T(8,128)(2,1)}, u32[]{:S(2)}) copy-start(bf16[256,512]{1,0:T(8,128)(2,1)} %param.8) | copy-start | bytes 786436
  153.8 7.2 %copy-start.3 = (bf16[512,512]{1,0:T(8,128)(2,1)S(1)}, bf16[512,512]{1,0:T(8,128)(2,1)}, u32[]{:S(2)}) copy-start(bf16[512,512]{1,0:T(8,128)(2,1)} %param.12) | copy-start | bytes 1572868
  159.1 2.2 copy-start.7
  159.2 2.5 copy-start.5
  159.2 2.5 copy-start.8
  165.2 2.8 copy-start.4
  167.9 319.9 %all-reduce.5.cloned.1.call-start = ((), (), s32[]{:S(2)}) async-start(), calls=%async_computation.3 | async-start | bytes 8388608 | tf_op jit(solution)/shard_map/psum | solution.py:7
  210.8 120.6 %collective-permute-start.3 = (bf16[4096,512]{1,0:T(8,128)(2,1)}, bf16[4096,512]{1,0:T(8,128)(2,1)}, u32[]{:S(2)}, u32[]{:S(2)}) collective-permute-start(bf16[4096,512]{1,0:T(8,128)(2,1)} %bitcast.13), channel_id=1, source_target_pairs={{0,16},{16,32},{32,48},{48,64},{64,80},{80,96},{96,112},{112,128},... | collective-permute-start | bytes 12582920 | tf_op jit(solution)/shard_map/ppermute | solution.py:13
  210.9 120.6 %collective-permute-start.2 = (bf16[4096,512]{1,0:T(8,128)(2,1)}, bf16[4096,512]{1,0:T(8,128)(2,1)}, u32[]{:S(2)}, u32[]{:S(2)}) collective-permute-start(bf16[4096,512]{1,0:T(8,128)(2,1)} %bitcast.12), channel_id=1, source_target_pairs={{0,240},{16,0},{32,16},{48,32},{64,48},{80,64},{96,80},{112,96},{1... | collective-permute-start | bytes 12582920 | tf_op jit(solution)/shard_map/ppermute | solution.py:13
  323.2 244.7 %reduce-scatter.2.cloned.1.call-start = ((), (), s32[]{:S(2)}) async-start(), calls=%async_computation.2 | async-start | bytes 4456448 | tf_op jit(solution)/shard_map/reduce_scatter | solution.py:72
  341.0 1.0 copy-start.9
  341.0 2.1 copy-start.6
  341.1 228.6 %copy-start.1 = (bf16[2,8,128,128]{3,2,1,0:T(8,128)(2,1)S(1)}, bf16[2,8,128,128]{3,2,1,0:T(8,128)(2,1)}, u32[]{:S(2)}) copy-start(bf16[2,8,128,128]{3,2,1,0:T(8,128)(2,1)} %param.9) | copy-start | bytes 1572868
Sparse Core Ops, SparseCore 0:
  9.8 79.7 all-gather.1
  168.0 155.1 all-reduce.6
  326.1 161.5 all-reduce.4
  490.1 77.7 reduce-scatter.1
